TPU v7x, 32 devices: a whole 2x2x4 slice. The times are simulated.
32 devices in a mesh: dom: 16 (over z, y, core), head: 2 (over x).
Axes of the slice: x: 2, y: 2, z: 4, core: 2. Of those that a mesh axis runs over, the one named last changes fastest.
Arguments:
- node_feats: bfloat16 [6144, 512], P('dom', 'head'), may hold values from -16 to 16
- tile_vals: bfloat16 [48, 4, 128, 128], P('dom'), may hold values from -0.375 to 0.375
- tile_counts: int32 [48], P('dom'), may hold values from 1 to 4
- tile_cols: int32 [48, 4], P('dom'), may hold values from 0 to 6
- send_rows: int32 [16, 4, 128], P('dom'), may hold values from 0 to 383, as said below
- w_msg: bfloat16 [512, 512], P(None, 'head'), may hold values from -0.25 to 0.25
- w_qkv: bfloat16 [3, 512, 512], P(None, None, 'head'), may hold values from -0.25 to 0.25
- w_out: bfloat16 [512, 512], P('head'), may hold values from -0.25 to 0.25
Outputs:
- updated: bfloat16 [6144, 512], P('dom', 'head')
Inputs may be any that keep to these rules, and one draw needn't show every extreme that they name: `send_rows`: local row indices within the sending partition. `tile_cols`: block c < 3 of a partition's row table is its own row block c; block 3 + j is the block of 128 rows received with offset index j.
All inputs are finite; a program needn't handle non-finite values.
Results may differ from a plain program's by a relative error of at most 0.012.
The roundings to bfloat16 on the way count: a program that leaves them out, or rounds other values in their place, can miss the bound.
Values may be sent and summed in bfloat16 or wider, within the bound.
A program may use at most 64 MiB of HBM per device.

v0:
```python
import math

import jax
import jax.numpy as jnp
from jax import lax
from jax.sharding import PartitionSpec as P

D = 512
H = 8
REACH = 2


def passed_along(block, axis, distance):
    devices = range(lax.axis_size(axis))
    route = [((i - distance) % len(devices), i) for i in devices]
    return lax.ppermute(block, axis, route)


def offsets(reach_count):
    return [
        position - reach_count if position < reach_count else position - reach_count + 1
        for position in range(2 * reach_count)
    ]


def boundary(row_table, send_rows):
    pieces = [row_table]
    for direction, shift_by in enumerate(offsets(REACH)):
        chosen = jnp.take(row_table, send_rows[0, direction], axis=0)
        pieces.append(passed_along(chosen, "dom", shift_by))
    return jnp.concatenate(pieces, axis=0)


def aggregate(row_table, tile_vals, tile_counts, tile_cols):
    block_rows = tile_vals.shape[2]
    columns = row_table.shape[1]
    blocks = row_table.reshape(-1, block_rows, columns)
    picked = jnp.take(blocks, tile_cols, axis=0)
    slots = lax.broadcasted_iota(jnp.int32, tile_cols.shape, 1)
    live = slots < tile_counts[:, None]
    masked = jnp.where(live[:, :, None, None], tile_vals, jnp.zeros_like(tile_vals))
    summed = jnp.einsum("rtij,rtjc->ric", masked, picked, preferred_element_type=jnp.float32)
    return summed.reshape(-1, columns).astype(jnp.bfloat16)


def make_fold(queries, head_count, depth):
    scale = 1.0 / math.sqrt(depth)

    def update(state, key_block, value_block):
        running, total, accum = state
        scores = (
            jnp.einsum("qhd,khd->hqk", queries, key_block, preferred_element_type=jnp.float32)
            * scale
        )
        newest = jnp.maximum(running, scores.max(axis=2))
        factor = jnp.exp(running - newest)
        weights = jnp.exp(scores - newest[:, :, None]).astype(jnp.bfloat16)
        total = total * factor + weights.astype(jnp.float32).sum(axis=2)
        accum = accum * factor[:, :, None] + jnp.einsum(
            "hqk,khd->hqd", weights, value_block, preferred_element_type=jnp.float32
        )
        return (newest, total, accum)

    def fold(state, pieces, start):
        key_piece, value_piece = pieces
        length = key_piece.shape[0]
        span = math.gcd(length, 2048)
        keys_blocked = key_piece.reshape(length // span, span, head_count, depth)
        values_blocked = value_piece.reshape(length // span, span, head_count, depth)

        def inner(carried, blocked):
            return (update(carried, blocked[0], blocked[1]), None)

        state, unused = lax.scan(inner, state, (keys_blocked, values_blocked))
        return state

    return fold


def local(node_feats, tile_vals, tile_counts, tile_cols, send_rows, w_msg, w_qkv, w_out):
    depth = D // H
    row_count = node_feats.shape[0]
    local_cols = node_feats.shape[1]
    head_count = local_cols // depth
    gathered = lax.all_gather(node_feats, "head", axis=1, tiled=True)
    query = jnp.dot(gathered, w_qkv[0], preferred_element_type=jnp.float32).astype(jnp.bfloat16)
    keys_local = jnp.dot(gathered, w_qkv[1], preferred_element_type=jnp.float32).astype(
        jnp.bfloat16
    )
    values_local = jnp.dot(gathered, w_qkv[2], preferred_element_type=jnp.float32).astype(
        jnp.bfloat16
    )
    queries = query.reshape(row_count, head_count, depth)
    start_state = (
        jnp.full((head_count, row_count), -1e30, jnp.float32),
        jnp.zeros((head_count, row_count), jnp.float32),
        jnp.zeros((head_count, row_count, depth), jnp.float32),
    )
    fold = make_fold(queries, head_count, depth)
    all_keys, all_values = (
        lax.all_gather(keys_local, "dom", axis=0, tiled=True),
        lax.all_gather(values_local, "dom", axis=0, tiled=True),
    )
    state = fold(start_state, (all_keys, all_values), 0)
    running, total, accum = state
    heads_out = (
        (accum / total[:, :, None])
        .transpose(1, 0, 2)
        .reshape(row_count, local_cols)
        .astype(jnp.bfloat16)
    )
    partial_value = jnp.dot(heads_out, w_out, preferred_element_type=jnp.float32)
    attended = lax.psum_scatter(partial_value, "head", scatter_dimension=1, tiled=True)
    row_table = boundary(gathered, send_rows)
    aggregated = aggregate(row_table, tile_vals, tile_counts, tile_cols)
    message = jnp.dot(aggregated, w_msg, preferred_element_type=jnp.float32)
    message = jnp.maximum(message, 0.0)
    return (node_feats.astype(jnp.float32) + message + attended).astype(jnp.bfloat16)


def solution(mesh):
    placed = (
        P("dom", "head"),
        P("dom", None, None, None),
        P("dom"),
        P("dom", None),
        P("dom", None, None),
        P(None, "head"),
        P(None, None, "head"),
        P("head", None),
    )
    return jax.shard_map(
        local, mesh=mesh, in_specs=placed, out_specs=P("dom", "head"), check_vma=False
    )
```

profile of v0, /device:TPU:0, one launch (start us, length us, event | category | flops | bytes accessed | tf_op | source)
XLA Modules:
  0.0 217.5 jit_solution(15187135193433598856)
XLA Ops:
  6.5 8.9 %all_gather.9 = bf16[384,512]{1,0:T(8,128)(2,1)S(1)} all-gather(bf16[384,256]{1,0:T(8,128)(2,1)} %param.12), channel_id=1, replica_groups=mesh['dom'=16,'head'=2] {'head'}, dimensions={1}, use_global_device_ids=true | all-gather | bytes 589824 | tf_op jit(solution)/shard_map/all_gather | solution.py:85
  15.4 1.9 convolution_convert_fusion.2
  17.4 1.9 convolution_convert_fusion
  20.2 0.8 gather_fusion.1
  21.2 4.8 %collective-permute-start = (bf16[128,512]{1,0:T(8,128)(2,1)S(1)}, bf16[128,512]{1,0:T(8,128)(2,1)S(1)}, u32[]{:S(2)}, u32[]{:S(2)}) collective-permute-start(bf16[128,512]{1,0:T(8,128)(2,1)S(1)} %broadcast_select_fusion.3), channel_id=1, source_target_pairs={{4,0},{6,2},{8,4},{10,6},{12,8},{14,10},{16,12},{18,14},{20,16},{2... | collective-permute-start | bytes 393224 | tf_op jit(solution)/shard_map/ppermute | solution.py:16
  27.0 0.8 gather_fusion.3
  28.5 0.8 gather_fusion.4
  29.4 1.3 convolution_convert_fusion.1
  30.7 36.0 %all-gather.3.cloned.1.call-done = bf16[6144,256]{1,0:T(8,128)(2,1)} async-done(((bf16[384,256]{1,0:T(8,128)(2,1)}), bf16[6144,256]{1,0:T(8,128)(2,1)}) %all-gather.3.cloned.1.call-update) | async-done | bytes 3145744 | tf_op jit(solution)/shard_map/all_gather | solution.py:101
  66.7 10.2 %reshape.107 = bf16[3,2048,4,64]{3,2,1,0:T(4,128)(2,1)} reshape(bf16[6144,256]{1,0:T(8,128)(2,1)} %all-gather.3.cloned.1.call-done) | data formatting | bytes 6291456 | tf_op jit(solution)/shard_map/reshape | solution.py:68
  76.9 9.9 %copy.15 = bf16[3,2048,4,64]{1,3,2,0:T(8,128)(2,1)} copy(bf16[3,2048,4,64]{3,2,1,0:T(4,128)(2,1)} %reshape.107) | data formatting | bytes 6291456
  86.8 26.2 %all-gather.5.cloned.1.call-done = bf16[6144,256]{1,0:T(8,128)(2,1)} async-done(((bf16[384,256]{1,0:T(8,128)(2,1)}), bf16[6144,256]{1,0:T(8,128)(2,1)}) %all-gather.5.cloned.1.call-update) | async-done | bytes 3145744 | tf_op jit(solution)/shard_map/all_gather | solution.py:102
  113.0 10.2 %reshape.108 = bf16[3,2048,4,64]{3,2,1,0:T(4,128)(2,1)} reshape(bf16[6144,256]{1,0:T(8,128)(2,1)} %all-gather.5.cloned.1.call-done) | data formatting | bytes 6291456 | tf_op jit(solution)/shard_map/reshape | solution.py:69
  123.2 9.9 %copy.16 = bf16[3,2048,4,64]{1,3,2,0:T(8,128)(2,1)} copy(bf16[3,2048,4,64]{3,2,1,0:T(4,128)(2,1)} %reshape.108) | data formatting | bytes 6291456
  133.1 58.1 %while.15 = (s32[]{:T(128)}, f32[4,384]{1,0:T(4,128)S(1)}, f32[4,384]{1,0:T(4,128)S(1)}, f32[4,384,64]{1,2,0:T(8,128)S(1)}, bf16[3,2048,4,64]{1,3,2,0:T(8,128)(2...) while((s32[]{:T(128)}, f32[4,384]{1,0:T(4,128)S(1)}, ...), condition=%wide.region_3.0_spmd.clone, body=%wide.region_0.0_spmd.clone.sunk | while | flops 837066240 | bytes 91260032 | solution.py:74
  133.1 7.6 %bitcast_reduce_fusion.2 = (f32[4,384]{1,0:T(4,128)S(1)}, f32[4,2048,384]{2,1,0:T(8,128)}) fusion(bf16[384,4,64]{0,2,1:T(8,128)(2,1)S(1)} %get-tuple-element.192, bf16[3,2048,4,64]{1,3,2,0:T(8,128)(2,1)} %get-tuple-element.191, s32[]{:T(128)} %get-tuple-element.178), kind=kOutput, calls=%fused_computation.6.clone.1 | convolution fusion | flops 408943104 | bytes 13834752 | tf_op jit(solution)/shard_map/while/body/eval_jaxpr/qhd,khd->hqk/dot_general | solution.py:52
  140.7 6.8 %convert_reduce_fusion.2 = f32[4,384]{1,0:T(4,128)S(1)} fusion(f32[4,384]{1,0:T(4,128)S(1)} %select_maximum_fusion.2, f32[4,2048,384]{2,1,0:T(8,128)} %get-tuple-element.166), kind=kLoop, calls=%fused_computation.9.clone.1 | loop fusion | flops 15727104 | bytes 12595200 | tf_op jit(solution)/shard_map/while/body/eval_jaxpr/reduce_sum | solution.py:58
  147.5 1.3 copy-done.1
  148.9 3.6 %convolution_add_fusion.2 = f32[4,384,64]{1,2,0:T(8,128)S(1)} fusion(bf16[3,2048,4,64]{1,3,2,0:T(8,128)(2,1)} %get-tuple-element.193, s32[]{:T(128)} %get-tuple-element.178, f32[4,2048,384]{2,1,0:T(8,128)S(1)} %copy-done.1, f32[4,384]{1,0:T(4,128)S(1)} %select_maximum_fusion.2, f32[4,384,64]{1,2,0:T(8,128)S(1)} %get-tuple-element.181, ...), kind=kOutput, calls=%fused_computation.10.clone.1 | convolution fusion | flops 412385280 | bytes 14430721 | tf_op jit(solution)/shard_map/while/body/eval_jaxpr/hqk,khd->hqd/dot_general | solution.py:59
  152.5 7.6 %bitcast_reduce_fusion.2 = (f32[4,384]{1,0:T(4,128)S(1)}, f32[4,2048,384]{2,1,0:T(8,128)}) fusion(bf16[384,4,64]{0,2,1:T(8,128)(2,1)S(1)} %get-tuple-element.192, bf16[3,2048,4,64]{1,3,2,0:T(8,128)(2,1)} %get-tuple-element.191, s32[]{:T(128)} %get-tuple-element.178), kind=kOutput, calls=%fused_computation.6.clone.1 | convolution fusion | flops 408943104 | bytes 13834752 | tf_op jit(solution)/shard_map/while/body/eval_jaxpr/qhd,khd->hqk/dot_general | solution.py:52
  160.1 6.8 %convert_reduce_fusion.2 = f32[4,384]{1,0:T(4,128)S(1)} fusion(f32[4,384]{1,0:T(4,128)S(1)} %select_maximum_fusion.2, f32[4,2048,384]{2,1,0:T(8,128)} %get-tuple-element.166), kind=kLoop, calls=%fused_computation.9.clone.1 | loop fusion | flops 15727104 | bytes 12595200 | tf_op jit(solution)/shard_map/while/body/eval_jaxpr/reduce_sum | solution.py:58
  166.9 1.3 copy-done.1
  168.2 3.6 %convolution_add_fusion.2 = f32[4,384,64]{1,2,0:T(8,128)S(1)} fusion(bf16[3,2048,4,64]{1,3,2,0:T(8,128)(2,1)} %get-tuple-element.193, s32[]{:T(128)} %get-tuple-element.178, f32[4,2048,384]{2,1,0:T(8,128)S(1)} %copy-done.1, f32[4,384]{1,0:T(4,128)S(1)} %select_maximum_fusion.2, f32[4,384,64]{1,2,0:T(8,128)S(1)} %get-tuple-element.181, ...), kind=kOutput, calls=%fused_computation.10.clone.1 | convolution fusion | flops 412385280 | bytes 14430721 | tf_op jit(solution)/shard_map/while/body/eval_jaxpr/hqk,khd->hqd/dot_general | solution.py:59
  171.8 7.6 %bitcast_reduce_fusion.2 = (f32[4,384]{1,0:T(4,128)S(1)}, f32[4,2048,384]{2,1,0:T(8,128)}) fusion(bf16[384,4,64]{0,2,1:T(8,128)(2,1)S(1)} %get-tuple-element.192, bf16[3,2048,4,64]{1,3,2,0:T(8,128)(2,1)} %get-tuple-element.191, s32[]{:T(128)} %get-tuple-element.178), kind=kOutput, calls=%fused_computation.6.clone.1 | convolution fusion | flops 408943104 | bytes 13834752 | tf_op jit(solution)/shard_map/while/body/eval_jaxpr/qhd,khd->hqk/dot_general | solution.py:52
  179.4 6.8 %convert_reduce_fusion.2 = f32[4,384]{1,0:T(4,128)S(1)} fusion(f32[4,384]{1,0:T(4,128)S(1)} %select_maximum_fusion.2, f32[4,2048,384]{2,1,0:T(8,128)} %get-tuple-element.166), kind=kLoop, calls=%fused_computation.9.clone.1 | loop fusion | flops 15727104 | bytes 12595200 | tf_op jit(solution)/shard_map/while/body/eval_jaxpr/reduce_sum | solution.py:58
  186.2 1.3 copy-done.1
  187.6 3.6 %convolution_add_fusion.2 = f32[4,384,64]{1,2,0:T(8,128)S(1)} fusion(bf16[3,2048,4,64]{1,3,2,0:T(8,128)(2,1)} %get-tuple-element.193, s32[]{:T(128)} %get-tuple-element.178, f32[4,2048,384]{2,1,0:T(8,128)S(1)} %copy-done.1, f32[4,384]{1,0:T(4,128)S(1)} %select_maximum_fusion.2, f32[4,384,64]{1,2,0:T(8,128)S(1)} %get-tuple-element.181, ...), kind=kOutput, calls=%fused_computation.10.clone.1 | convolution fusion | flops 412385280 | bytes 14430721 | tf_op jit(solution)/shard_map/while/body/eval_jaxpr/hqk,khd->hqd/dot_general | solution.py:59
  191.3 1.2 fusion.36
  193.5 7.5 %collective-permute-done.3 = bf16[128,512]{1,0:T(8,128)(2,1)S(1)} collective-permute-done((bf16[128,512]{1,0:T(8,128)(2,1)S(1)}, bf16[128,512]{1,0:T(8,128)(2,1)S(1)}, u32[]{:S(2)}, u32[]{:S(2)}) %collective-permute-start.3) | collective-permute-done | bytes 131104 | tf_op jit(solution)/shard_map/ppermute | solution.py:16
  201.6 1.5 fusion.18
  203.1 5.8 %reduce-scatter.2.cloned.1.call-done = f32[384,256]{1,0:T(8,128)} async-done(((f32[384,512]{1,0:T(8,128)}), f32[384,256]{1,0:T(8,128)}) %reduce-scatter.2.cloned.1.call-update) | async-done | bytes 393232 | tf_op jit(solution)/shard_map/reduce_scatter | solution.py:113
  208.9 2.0 fusion.23
  (56 shorter events, 4.4 us)
Async XLA Ops:
  6.5 184.7 %copy-start = (bf16[256,512]{1,0:T(8,128)(2,1)S(1)}, bf16[256,512]{1,0:T(8,128)(2,1)}, u32[]{:S(2)}) copy-start(bf16[256,512]{1,0:T(8,128)(2,1)} %param.19) | copy-start | bytes 786436
  6.5 60.2 %all-gather.3.cloned.1.call-start = ((), (), s32[]{:S(2)}) async-start(), calls=%async_computation.1 | async-start | bytes 3342336 | tf_op jit(solution)/shard_map/all_gather | solution.py:101
  17.3 95.7 %all-gather.5.cloned.1.call-start = ((), (), s32[]{:S(2)}) async-start(), calls=%async_computation.2 | async-start | bytes 3342336 | tf_op jit(solution)/shard_map/all_gather | solution.py:102
  19.3 189.6 %reduce-scatter.2.cloned.1.call-start = ((), (), s32[]{:S(2)}) async-start(), calls=%async_computation.3 | async-start | bytes 1179648 | tf_op jit(solution)/shard_map/reduce_scatter | solution.py:113
  21.2 172.2 %collective-permute-start = (bf16[128,512]{1,0:T(8,128)(2,1)S(1)}, bf16[128,512]{1,0:T(8,128)(2,1)S(1)}, u32[]{:S(2)}, u32[]{:S(2)}) collective-permute-start(bf16[128,512]{1,0:T(8,128)(2,1)S(1)} %broadcast_select_fusion.3), channel_id=1, source_target_pairs={{4,0},{6,2},{8,4},{10,6},{12,8},{14,10},{16,12},{18,14},{20,16},{2... | collective-permute-start | bytes 393224 | tf_op jit(solution)/shard_map/ppermute | solution.py:16
  27.0 166.5 %collective-permute-start.1 = (bf16[128,512]{1,0:T(8,128)(2,1)S(1)}, bf16[128,512]{1,0:T(8,128)(2,1)S(1)}, u32[]{:S(2)}, u32[]{:S(2)}) collective-permute-start(bf16[128,512]{1,0:T(8,128)(2,1)S(1)} %broadcast_select_fusion.2), channel_id=1, source_target_pairs={{2,0},{4,2},{6,4},{8,6},{10,8},{12,10},{14,12},{16,14},{18,16},{20... | collective-permute-start | bytes 393224 | tf_op jit(solution)/shard_map/ppermute | solution.py:16
  28.0 165.5 %collective-permute-start.2 = (bf16[128,512]{1,0:T(8,128)(2,1)S(1)}, bf16[128,512]{1,0:T(8,128)(2,1)S(1)}, u32[]{:S(2)}, u32[]{:S(2)}) collective-permute-start(bf16[128,512]{1,0:T(8,128)(2,1)S(1)} %broadcast_select_fusion.1), channel_id=1, source_target_pairs={{30,0},{0,2},{2,4},{4,6},{6,8},{8,10},{10,12},{12,14},{14,16},{16,... | collective-permute-start | bytes 393224 | tf_op jit(solution)/shard_map/ppermute | solution.py:16
  133.1 60.1 %copy-start.3 = (s32[3,4]{1,0:T(4,128)S(1)}, s32[3,4]{1,0:T(4,128)}, u32[]{:S(2)}) copy-start(s32[3,4]{1,0:T(4,128)} %param.15) | copy-start | bytes 148
  133.1 60.1 %copy-start.4 = (s32[3]{0:T(128)S(1)}, s32[3]{0:T(128)}, u32[]{:S(2)}) copy-start(s32[3]{0:T(128)} %param.14) | copy-start | bytes 40
  140.7 8.2 %copy-start.1 = (f32[4,2048,384]{2,1,0:T(8,128)S(1)}, f32[4,2048,384]{2,1,0:T(8,128)}, u32[]{:S(2)}) copy-start(f32[4,2048,384]{2,1,0:T(8,128)} %get-tuple-element.166) | copy-start | bytes 37748740 | tf_op jit(solution)/shard_map/while
  160.1 8.2 %copy-start.1 = (f32[4,2048,384]{2,1,0:T(8,128)S(1)}, f32[4,2048,384]{2,1,0:T(8,128)}, u32[]{:S(2)}) copy-start(f32[4,2048,384]{2,1,0:T(8,128)} %get-tuple-element.166) | copy-start | bytes 37748740 | tf_op jit(solution)/shard_map/while
  179.4 8.2 %copy-start.1 = (f32[4,2048,384]{2,1,0:T(8,128)S(1)}, f32[4,2048,384]{2,1,0:T(8,128)}, u32[]{:S(2)}) copy-start(f32[4,2048,384]{2,1,0:T(8,128)} %get-tuple-element.166) | copy-start | bytes 37748740 | tf_op jit(solution)/shard_map/while
  191.2 17.7 %copy-start.2 = (bf16[384,256]{1,0:T(8,128)(2,1)S(1)}, bf16[384,256]{1,0:T(8,128)(2,1)}, u32[]{:S(2)}) copy-start(bf16[384,256]{1,0:T(8,128)(2,1)} %param.12) | copy-start | bytes 589828
  192.6 8.4 %collective-permute-start.3 = (bf16[128,512]{1,0:T(8,128)(2,1)S(1)}, bf16[128,512]{1,0:T(8,128)(2,1)S(1)}, u32[]{:S(2)}, u32[]{:S(2)}) collective-permute-start(bf16[128,512]{1,0:T(8,128)(2,1)S(1)} %broadcast_select_fusion), channel_id=1, source_target_pairs={{28,0},{30,2},{0,4},{2,6},{4,8},{6,10},{8,12},{10,14},{12,16},{14,... | collective-permute-start | bytes 393224 | tf_op jit(solution)/shard_map/ppermute | solution.py:16
Sparse Core Ops, SparseCore 0:
  17.5 49.2 all-gather.2
  69.0 44.0 all-gather.4
  192.6 16.2 reduce-scatter.1
where the time goes:
time: 219 us; the launch traced here: 217 us
  waiting for transfers between devices  75.7 us (35%)
  local copies, waits for them, and re-layouts  48.4 us (22%)
  matrix products  43.3 us (20%)
  other arithmetic  21.8 us (10%)
  between operations  13.3 us (6%)
  blocking collectives  8.89 us (4%)
  starting transfers between devices  6.1 us (3%)
    all_gather x1, waiting for transfers between devices, local(): lax.all_gather(keys_local, 'dom', axis=0, tiled=True)  36 us
    all_gather x1, waiting for transfers between devices, local(): lax.all_gather(values_local, 'dom', axis=0, tiled=True)  26.2 us
    dot_general x3, matrix products, update(): jnp.einsum('qhd,khd->hqk', queries, key_block, preferred_element_type=jnp...  22.8 us
    reduce_sum x3, other arithmetic, update(): total = total * factor + weights.astype(jnp.float32).sum(axis=2)  20.3 us
    unnamed x14, local copies, waits for them, and re-layouts  19.8 us
    dot_general x3, matrix products, update(): jnp.einsum('hqk,khd->hqd', weights, value_block, preferred_element_type=j...  10.7 us
    reshape x1, local copies, waits for them, and re-layouts, fold(): keys_blocked = key_piece.reshape(length // span, span, head_count, depth)  10.2 us
    reshape x1, local copies, waits for them, and re-layouts, fold(): value_piece.reshape(length // span, span, head_count, depth)  10.2 us
  transfers between devices with their start and end apart: 7, of which 4 were waited for; matrix products, arithmetic and copies ran while one was open for 48% of the time, Pallas kernels for 0%

commit v1 on v0

v1 whole, which is shorter than its diff:
```python
import functools
import math

import jax
import jax.numpy as jnp
from jax import lax
from jax.experimental import pallas as pl
from jax.experimental.pallas import tpu as pltpu
from jax.sharding import PartitionSpec as P

DEPTH = 64
LANES = 128
MESH = pl.DeviceIdType.MESH
F32 = jnp.float32
BF16 = jnp.bfloat16


def offsets(count):
    reach = count // 2
    return [j - reach if j < reach else j - reach + 1 for j in range(count)]


def ring_next(chip, chips, step):
    depth = 4 if chips % 4 == 0 else 2
    width = chips // depth
    z, y = chip // width, chip % width
    if width == 1:
        return (chip + step + chips) % chips
    k = depth - 1 - z
    inner = width - 1
    odd = k % 2
    along = (1 - odd) * (y - 1) + odd * (width - 1 - y)
    first = 1 - jnp.minimum(y, 1)
    at = first * z + (1 - first) * (depth + k * inner + along)
    at = (at + step + chips) % chips
    far = 1 - jnp.minimum(jnp.maximum(at - (depth - 1), 0), 1)
    rest = jnp.maximum(at - depth, 0)
    k2 = rest // inner
    a2 = rest % inner
    odd2 = k2 % 2
    y2 = (1 - odd2) * (a2 + 1) + odd2 * (width - 1 - a2)
    z2 = depth - 1 - k2
    return far * (at * width) + (1 - far) * (z2 * width + y2)


def body(
    ndom, nhead, scale,
    live_ref, x_ref, tiles_ref, rows_ref, wmsg_ref, wqkv_ref, wout_ref,
    out_ref,
    table, chosen, wsend, wo, kv, qs, mx, acc, hg, msg,
    x_send, x_recv, w_send, w_recv, b_send, b_recv,
    r_send, r_recv, s_send, s_recv, h_send, h_recv,
):
    rows, cols = x_ref.shape
    width = qs.shape[2] * (kv.shape[3] // (2 * LANES))
    heads = qs.shape[0]
    half = rows // 2
    chips = ndom // 2
    steps = chips // 2
    blk = tiles_ref.shape[2]
    row_blocks, slots = tiles_ref.shape[0], tiles_ref.shape[1]
    reach = rows_ref.shape[0]
    blocks = row_blocks + reach
    me = lax.axis_index("dom")
    hd = lax.axis_index("head")
    chip, core = me // 2, me % 2
    right = (ring_next(chip, chips, 1) * 2 + core, hd)
    left = (ring_next(chip, chips, -1) * 2 + core, hd)
    sib = (chip * 2 + 1 - core, hd)
    near = [((me + o + ndom) % ndom, hd) for o in offsets(reach)]
    peers = [(me, (hd + k) % nhead) for k in range(1, nhead)]

    barrier = pltpu.get_barrier_semaphore()
    everyone = [right, left, sib] + near + peers
    for d in everyone:
        pl.semaphore_signal(barrier, inc=1, device_id=d, device_id_type=MESH)

    for k in range(nhead):
        wsend[k] = wout_ref[:, k * cols:(k + 1) * cols]
    table[hd, pl.ds(0, rows), :] = x_ref[...]
    pl.semaphore_wait(barrier, len(everyone))

    def copy(src, dst, ss, rs, to):
        return pltpu.make_async_remote_copy(
            src_ref=src, dst_ref=dst, send_sem=ss, recv_sem=rs, device_id=to, device_id_type=MESH
        )

    def x_copy(k):
        return copy(x_ref, table.at[hd, pl.ds(0, rows)], x_send.at[k], x_recv.at[k], peers[k])

    def w_copy(k):
        to = (hd + k + 1) % nhead
        return copy(wsend.at[to], wo.at[hd], w_send.at[k], w_recv.at[k], peers[k])

    def h_copy(k):
        return copy(hg.at[hd], hg.at[hd], h_send.at[k], h_recv.at[k], peers[k])

    def b_copy(j):
        dst = table.at[:, pl.ds(rows + j * blk, blk)]
        return copy(chosen.at[j], dst, b_send.at[j], b_recv.at[j], near[j])

    def part(ch):
        return pl.ds(ch * half, half)

    def ring_copy(s, way, ch):
        to = right if way == 0 else left
        if isinstance(s, int) and s == 1:
            src = kv.at[0, 0, part(ch)]
        else:
            src = kv.at[2 * s - 2, way, part(ch)]
        if isinstance(s, int) and s == steps:
            dst = kv.at[1, 0, part(ch)]
        else:
            dst = kv.at[2 * s, way, part(ch)]
        return copy(src, dst, r_send.at[s, way, ch], r_recv.at[s, way, ch], to)

    def sib_copy(s, way, ch):
        if isinstance(s, int) and s == 0:
            src, dst = kv.at[0, 0, part(ch)], kv.at[0, 1, part(ch)]
        elif isinstance(s, int) and s == steps:
            src, dst = kv.at[1, 0, part(ch)], kv.at[1, 1, part(ch)]
        else:
            src, dst = kv.at[2 * s, way, part(ch)], kv.at[2 * s + 1, way, part(ch)]
        return copy(src, dst, s_send.at[s, way, ch], s_recv.at[s, way, ch], sib)

    for k in range(nhead - 1):
        x_copy(k).start()

    def project(which, k, rs):
        w = wqkv_ref[which, pl.ds(pl.multiple_of(k * cols, cols), cols), :]
        x = table[k, rs, :]
        return jnp.dot(x, w, preferred_element_type=F32)

    def tiled(value, h):
        t = h // 2
        return value[:, t * LANES:(t + 1) * LANES]

    wo[hd] = wsend[hd]
    for h in range(heads):
        mx[h] = jnp.full((rows, LANES), -1e30, F32)
        acc[h] = jnp.zeros((rows, LANES), F32)

    whole = pl.ds(0, rows)
    begun = [project(i, hd, whole) for i in (1, 2)]
    for k in range(nhead - 1):
        x_copy(k).wait_recv()
        w_copy(k).start()
    for k in range(1, nhead):
        other = (hd + k) % nhead
        begun = [b + project(i, other, whole) for b, i in zip(begun, (1, 2))]
    for ch in range(2):
        for i in range(2):
            kv[0, 0, part(ch), i * width:(i + 1) * width] = begun[i][ch * half:(ch + 1) * half].astype(BF16)
        for way in range(2):
            ring_copy(1, way, ch).start()
        sib_copy(0, 0, ch).start()

    lane = lax.broadcasted_iota(jnp.int32, (1, LANES), 1)

    def mine(h):
        return (lane // DEPTH) == (h % 2)

    query = project(0, hd, whole)
    for k in range(1, nhead):
        query = query + project(0, (hd + k) % nhead, whole)
    query = query.astype(BF16)
    for h in range(heads):
        tile = tiled(query, h)
        qs[h] = jnp.where(mine(h), tile, jnp.zeros_like(tile))

    line = lax.broadcasted_iota(jnp.int32, (rows, blk), 0)
    for j in range(reach):
        pick = jnp.where(line == rows_ref[j:j + 1, :], 1.0, 0.0).astype(BF16)
        for k in range(nhead):
            got = lax.dot_general(
                pick, table[k, pl.ds(0, rows), :], (((0,), (0,)), ((), ())), preferred_element_type=F32
            )
            chosen[j, k] = got.astype(BF16)
        b_copy(j).start()

    factor = scale * math.log2(math.e)

    def attend(at):
        for h in range(heads):
            t = h // 2
            keys = kv[at, :, :, t * LANES:(t + 1) * LANES].reshape(2 * rows, LANES)
            values = kv[at, :, :, width + t * LANES:width + (t + 1) * LANES].reshape(2 * rows, LANES)
            values = jnp.where(mine(h), values, jnp.ones_like(values))
            s = lax.dot_general(qs[h], keys, (((1,), (1,)), ((), ())), preferred_element_type=F32)
            old = mx[h]
            new = jnp.maximum(old, jnp.max(s, axis=1, keepdims=True))
            p = jnp.exp2((s - new[:, :1]) * factor).astype(BF16)
            acc[h] = acc[h] * jnp.exp2((old - new) * factor) + jnp.dot(
                p, values, preferred_element_type=F32
            )
            mx[h] = new

    for ch in range(2):
        sib_copy(0, 0, ch).wait_recv()
    attend(0)

    def arrive(s, last):
        for ch in range(2):
            for way in range(2):
                ring_copy(s, way, ch).wait_recv()
                if not last or way == ch:
                    ring_copy_next(s, way, ch, last).start()
                sib_copy(s, way, ch).start()

    def ring_copy_next(s, way, ch, last):
        if last:
            return ring_copy(steps, way, ch)
        return ring_copy(s + 1, way, ch)

    def taken(s):
        for ch in range(2):
            for way in range(2):
                sib_copy(s, way, ch).wait_recv()

    def turn(i, carry):
        s = i + 1
        arrive(s, False)
        attend(2 * s)
        taken(s)
        attend(2 * s + 1)
        return carry

    lax.fori_loop(0, steps - 2, turn, 0)

    s = steps - 1
    arrive(s, True)
    for j in range(reach):
        b_copy(j).wait_recv()
    for r in range(row_blocks):
        total = [jnp.zeros((blk, cols), F32) for _ in range(nhead)]
        for t in range(slots):
            tile = tiles_ref[r, t]
            place = live_ref[r * slots + t:r * slots + t + 1, :]
            spread = jnp.concatenate(
                [tile * jnp.where(place == b, 1.0, 0.0).astype(BF16) for b in range(blocks)], axis=1
            )
            for k in range(nhead):
                total[k] = total[k] + jnp.dot(spread, table[k], preferred_element_type=F32)
        sent = jnp.zeros((blk, cols), F32)
        for k in range(nhead):
            sent = sent + jnp.dot(
                total[k].astype(BF16), wmsg_ref[k * cols:(k + 1) * cols, :], preferred_element_type=F32
            )
        msg[r * blk:(r + 1) * blk, :] = jnp.maximum(sent, 0.0) + x_ref[r * blk:(r + 1) * blk, :].astype(F32)
    attend(2 * s)
    for ch in range(2):
        ring_copy(steps, ch, ch).wait_recv()
        sib_copy(steps, 0, ch).start()
    taken(s)
    attend(2 * s + 1)
    for ch in range(2):
        sib_copy(steps, 0, ch).wait_recv()
    attend(1)

    for t in range((heads + 1) // 2):
        made = jnp.zeros((rows, LANES), F32)
        for h in range(2 * t, min(2 * t + 2, heads)):
            a = acc[h]
            made = jnp.where(mine(h), a / pltpu.roll(a, DEPTH, 1), made)
        hg[hd, :, t * LANES:(t + 1) * LANES] = made.astype(BF16)
    for k in range(nhead - 1):
        h_copy(k).start()
    result = msg[...] + jnp.dot(hg[hd], wo[hd], preferred_element_type=F32)
    for k in range(nhead - 1):
        w_copy(k).wait_recv()
        h_copy(k).wait_recv()
    for k in range(1, nhead):
        other = (hd + k) % nhead
        result = result + jnp.dot(hg[other], wo[other], preferred_element_type=F32)
    out_ref[...] = result.astype(BF16)

    for k in range(nhead - 1):
        x_copy(k).wait_send()
        w_copy(k).wait_send()
        h_copy(k).wait_send()
    for j in range(reach):
        b_copy(j).wait_send()
    for ch in range(2):
        sib_copy(0, 0, ch).wait_send()
        sib_copy(steps, 0, ch).wait_send()
        ring_copy(steps, ch, ch).wait_send()
        for way in range(2):
            ring_copy(1, way, ch).wait_send()

    def sent_all(i, carry):
        for ch in range(2):
            for way in range(2):
                sib_copy(i + 1, way, ch).wait_send()
        return carry

    def sent_ring(i, carry):
        for ch in range(2):
            for way in range(2):
                ring_copy(i + 2, way, ch).wait_send()
        return carry

    lax.fori_loop(0, steps - 1, sent_all, 0)
    lax.fori_loop(0, steps - 2, sent_ring, 0)


def local(ndom, nhead, node_feats, tile_vals, tile_counts, tile_cols, send_rows, w_msg, w_qkv, w_out):
    rows, cols = node_feats.shape
    blk = tile_vals.shape[2]
    reach = send_rows.shape[1]
    heads = cols // DEPTH
    width = -(-cols // LANES) * LANES
    if width != cols:
        w_qkv = jnp.pad(w_qkv, ((0, 0), (0, 0), (0, width - cols)))
        w_out = jnp.pad(w_out, ((0, width - cols), (0, 0)))
    steps = ndom // 4
    dma = pltpu.SemaphoreType.DMA
    others = max(nhead - 1, 1)
    vmem = pl.BlockSpec(memory_space=pltpu.VMEM)
    slot = lax.broadcasted_iota(jnp.int32, tile_cols.shape, 1)
    live = jnp.where(slot < tile_counts[:, None], tile_cols, -1).reshape(-1, 1)
    live = jnp.broadcast_to(live, (live.shape[0], blk))
    return pl.pallas_call(
        functools.partial(body, ndom, nhead, 1.0 / math.sqrt(DEPTH)),
        out_shape=jax.ShapeDtypeStruct((rows, cols), BF16),
        in_specs=[vmem] * 7,
        out_specs=vmem,
        scratch_shapes=[
            pltpu.VMEM((nhead, rows + reach * blk, cols), BF16),
            pltpu.VMEM((reach, nhead, blk, cols), BF16),
            pltpu.VMEM((nhead, width, cols), BF16),
            pltpu.VMEM((nhead, width, cols), BF16),
            pltpu.VMEM((2 * steps, 2, rows, 2 * width), BF16),
            pltpu.VMEM((heads, rows, LANES), BF16),
            pltpu.VMEM((heads, rows, LANES), F32),
            pltpu.VMEM((heads, rows, LANES), F32),
            pltpu.VMEM((nhead, rows, width), BF16),
            pltpu.VMEM((rows, cols), F32),
            dma((others,)), dma((others,)),
            dma((others,)), dma((others,)),
            dma((reach,)), dma((reach,)),
            dma((steps + 1, 2, 2)), dma((steps + 1, 2, 2)),
            dma((steps + 1, 2, 2)), dma((steps + 1, 2, 2)),
            dma((others,)), dma((others,)),
        ],
        compiler_params=pltpu.CompilerParams(
            collective_id=0, has_side_effects=True, vmem_limit_bytes=48 * 1024 * 1024
        ),
    )(live, node_feats, tile_vals, send_rows[0], w_msg, w_qkv, w_out)


def solution(mesh):
    placed = (
        P("dom", "head"),
        P("dom", None, None, None),
        P("dom"),
        P("dom", None),
        P("dom", None, None),
        P(None, "head"),
        P(None, None, "head"),
        P("head", None),
    )
    return jax.shard_map(
        functools.partial(local, mesh.shape["dom"], mesh.shape["head"]),
        mesh=mesh, in_specs=placed, out_specs=P("dom", "head"), check_vma=False,
    )
```

time: 219 us -> 70.9 us (0.32)
  waiting for transfers between devices: 75.7 us -> 0 us
  Pallas kernels: 0 us -> 62.6 us
  matrix products: 43.3 us -> 0 us
  local copies, waits for them, and re-layouts: 48.4 us -> 7.05 us
  other arithmetic: 21.8 us -> 0.75 us
  between operations: 13.3 us -> 0.02 us
  blocking collectives: 8.89 us -> 0 us
  starting transfers between devices: 6.1 us -> 0 us
    pallas_call x0 -> x1, Pallas kernels: none -> 62.6 us  [local(): pl.pallas_call(functools.partial(body, ndom, nhead, 1.0 / math.sqrt(DEPTH...]
    all_gather x2 -> x0, waiting for transfers between devices: 62.3 us -> none  [the longest x1 36 us: local(): lax.all_gather(keys_local, 'dom', axis=0, tiled=True)]
    dot_general x12 -> x0, matrix products: 43.3 us -> none  [the longest x3 22.8 us: update(): jnp.einsum('qhd,khd->hqk', queries, key_block, preferred_element_type=jnp...]
    reshape x2 -> x0, local copies, waits for them, and re-layouts: 20.4 us -> none  [the longest x1 10.2 us: fold(): keys_blocked = key_piece.reshape(length // span, span, head_count, depth)]
    reduce_sum x3 -> x0, other arithmetic: 20.3 us -> none  [update(): total = total * factor + weights.astype(jnp.float32).sum(axis=2)]
    unnamed x14 -> x15, local copies, waits for them, and re-layouts: 19.8 us -> 6.9 us
    all_gather x1 -> x0, blocking collectives: 8.89 us -> none  [local(): gathered = lax.all_gather(node_feats, 'head', axis=1, tiled=True)]
    ppermute x4 -> x0, waiting for transfers between devices: 7.52 us -> none  [passed_along(): return lax.ppermute(block, axis, route)]
  transfers between devices with their start and end apart: 7 -> 0, of which waited for: 4 -> 0; matrix products, arithmetic and copies ran while one was open for 48% -> 0% of each run, Pallas kernels for 0% -> 0%
where the time goes in v1:
time: 70.9 us; the launch traced here: 70.4 us
  Pallas kernels  62.6 us (88%)
  local copies, waits for them, and re-layouts  7.05 us (10%)
  other arithmetic  0.75 us (1%)
    pallas_call x1, Pallas kernels, local(): pl.pallas_call(functools.partial(body, ndom, nhead, 1.0 / math.sqrt(DEPTH...  62.6 us
    unnamed x15, local copies, waits for them, and re-layouts  6.9 us

profile of v1, /device:TPU:0, one launch (start us, length us, event | category | flops | bytes accessed | tf_op | source)
XLA Modules:
  0.0 70.4 jit_solution(9475398236070162317)
XLA Ops:
  0.0 0.0 copy-start.6
  0.0 0.7 copy-done.6
  0.7 0.8 %fusion = s32[3,4]{1,0:T(4,128)S(1)} fusion(s32[3,4]{1,0:T(4,128)} %param.11, s32[3]{0:T(128)S(1)} %copy-done.6), kind=kLoop, calls=%fused_computation.1 | loop fusion | flops 24 | bytes 108 | tf_op jit(solution)/shard_map/jit(_where)/select_n | solution.py:320
  1.4 0.1 broadcast_in_dim.13
  1.5 0.0 copy-start.5
  1.5 0.1 broadcast_in_dim.14.live_ref
  1.6 0.6 copy-done.5
  2.2 0.0 copy-start
  2.2 1.1 %copy-done = bf16[3,512,256]{2,1,0:T(8,128)(2,1)S(1)} copy-done((bf16[3,512,256]{2,1,0:T(8,128)(2,1)S(1)}, bf16[3,512,256]{2,1,0:T(8,128)(2,1)}, u32[]{:S(2)}) %copy-start) | copy-done | bytes 786456
  3.3 0.0 copy-start.1
  3.3 1.0 %copy-done.1 = bf16[3,4,128,128]{3,2,1,0:T(8,128)(2,1)S(1)} copy-done((bf16[3,4,128,128]{3,2,1,0:T(8,128)(2,1)S(1)}, bf16[3,4,128,128]{3,2,1,0:T(8,128)(2,1)}, u32[]{:S(2)}) %copy-start.1) | copy-done | bytes 393240
  4.3 0.0 copy-start.2
  4.3 0.9 %copy-done.2 = bf16[512,256]{1,0:T(8,128)(2,1)S(1)} copy-done((bf16[512,256]{1,0:T(8,128)(2,1)S(1)}, bf16[512,256]{1,0:T(8,128)(2,1)}, u32[]{:S(2)}) %copy-start.2) | copy-done | bytes 262168
  5.3 0.0 copy-start.3
  5.3 0.9 %copy-done.3 = bf16[256,512]{1,0:T(8,128)(2,1)S(1)} copy-done((bf16[256,512]{1,0:T(8,128)(2,1)S(1)}, bf16[256,512]{1,0:T(8,128)(2,1)}, u32[]{:S(2)}) %copy-start.3) | copy-done | bytes 262168
  6.2 0.0 copy-start.4
  6.2 0.9 %copy-done.4 = bf16[384,256]{1,0:T(8,128)(2,1)S(1)} copy-done((bf16[384,256]{1,0:T(8,128)(2,1)S(1)}, bf16[384,256]{1,0:T(8,128)(2,1)}, u32[]{:S(2)}) %copy-start.4) | copy-done | bytes 196632
  7.1 62.6 %shard_map.82 = bf16[384,256]{1,0:T(8,128)(2,1)S(1)} custom-call(s32[12,128]{1,0:T(8,128)S(1)} %broadcast_in_dim.14.live_ref, bf16[384,256]{1,0:T(8,128)(2,1)S(1)} %copy-done.4, bf16[3,4,128,128]{3,2,1,0:T(8,128)(2,1)S(1)} %copy-done.1, s32[4,128]{1,0:T(4,128)S(1)} %bitcast.1, bf16[512,256]{1,0:T(8,128)(2,1)S(1)} %copy-done.2, ...), custom_call_target="tpu_custom_call" | custom-call | tf_op jit(solution)/shard_map/pallas_call | solution.py:322
  69.8 0.7 copy.10
Async XLA Ops:
  0.0 0.7 copy-start.6
  1.5 0.7 copy-start.5
  2.2 1.1 %copy-start = (bf16[3,512,256]{2,1,0:T(8,128)(2,1)S(1)}, bf16[3,512,256]{2,1,0:T(8,128)(2,1)}, u32[]{:S(2)}) copy-start(bf16[3,512,256]{2,1,0:T(8,128)(2,1)} %wqkv_ref.1) | copy-start | bytes 2359300
  3.3 1.0 %copy-start.1 = (bf16[3,4,128,128]{3,2,1,0:T(8,128)(2,1)S(1)}, bf16[3,4,128,128]{3,2,1,0:T(8,128)(2,1)}, u32[]{:S(2)}) copy-start(bf16[3,4,128,128]{3,2,1,0:T(8,128)(2,1)} %tiles_ref.1) | copy-start | bytes 1179652
  4.3 0.9 %copy-start.2 = (bf16[512,256]{1,0:T(8,128)(2,1)S(1)}, bf16[512,256]{1,0:T(8,128)(2,1)}, u32[]{:S(2)}) copy-start(bf16[512,256]{1,0:T(8,128)(2,1)} %wmsg_ref.1) | copy-start | bytes 786436
  5.3 0.9 %copy-start.3 = (bf16[256,512]{1,0:T(8,128)(2,1)S(1)}, bf16[256,512]{1,0:T(8,128)(2,1)}, u32[]{:S(2)}) copy-start(bf16[256,512]{1,0:T(8,128)(2,1)} %wout_ref.1) | copy-start | bytes 786436
  6.2 0.9 %copy-start.4 = (bf16[384,256]{1,0:T(8,128)(2,1)S(1)}, bf16[384,256]{1,0:T(8,128)(2,1)}, u32[]{:S(2)}) copy-start(bf16[384,256]{1,0:T(8,128)(2,1)} %x_ref.1) | copy-start | bytes 589828

commit v2 on v1

--- a/solution.py
+++ b/solution.py
@@ -45,10 +45,11 @@
 
 def body(
     ndom, nhead, scale,
-    live_ref, x_ref, tiles_ref, rows_ref, wmsg_ref, wqkv_ref, wout_ref,
+    live_in, x_ref, tiles_in, rows_in, wmsg_in, wqkv_in, wout_in,
     out_ref,
+    live_ref, tiles_ref, rows_ref, wmsg_ref, wqkv_ref, wout_ref, in_sem,
     table, chosen, wsend, wo, kv, qs, mx, acc, hg, msg,
-    x_send, x_recv, w_send, w_recv, b_send, b_recv,
+    x_send, x_recv, w_send, w_recv, b_send, b_recv, c_send, c_recv,
     r_send, r_recv, s_send, s_recv, h_send, h_recv,
 ):
     rows, cols = x_ref.shape
@@ -75,9 +76,18 @@
     for d in everyone:
         pl.semaphore_signal(barrier, inc=1, device_id=d, device_id_type=MESH)
 
-    for k in range(nhead):
-        wsend[k] = wout_ref[:, k * cols:(k + 1) * cols]
-    table[hd, pl.ds(0, rows), :] = x_ref[...]
+    def fetch(i, src, dst):
+        return pltpu.make_async_copy(src, dst, in_sem.at[i])
+
+    get_x = fetch(0, x_ref, table.at[hd, pl.ds(0, rows)])
+    get_qkv = fetch(1, wqkv_in, wqkv_ref)
+    get_rows = fetch(2, rows_in, rows_ref)
+    get_out = fetch(3, wout_in, wout_ref)
+    get_live = fetch(4, live_in, live_ref)
+    get_msg = fetch(5, wmsg_in, wmsg_ref)
+    get_tiles = fetch(6, tiles_in, tiles_ref)
+    for get in (get_x, get_qkv, get_rows, get_out, get_live, get_msg, get_tiles):
+        get.start()
     pl.semaphore_wait(barrier, len(everyone))
 
     def copy(src, dst, ss, rs, to):
@@ -96,8 +106,12 @@
         return copy(hg.at[hd], hg.at[hd], h_send.at[k], h_recv.at[k], peers[k])
 
     def b_copy(j):
-        dst = table.at[:, pl.ds(rows + j * blk, blk)]
+        dst = table.at[hd, pl.ds(rows + j * blk, blk)]
         return copy(chosen.at[j], dst, b_send.at[j], b_recv.at[j], near[j])
+
+    def c_copy(j, k):
+        both = table.at[hd, pl.ds(rows + j * blk, blk)]
+        return copy(both, both, c_send.at[j, k], c_recv.at[j, k], peers[k])
 
     def part(ch):
         return pl.ds(ch * half, half)
@@ -135,16 +149,16 @@
         t = h // 2
         return value[:, t * LANES:(t + 1) * LANES]
 
-    wo[hd] = wsend[hd]
     for h in range(heads):
         mx[h] = jnp.full((rows, LANES), -1e30, F32)
         acc[h] = jnp.zeros((rows, LANES), F32)
 
+    get_x.wait()
+    get_qkv.wait()
     whole = pl.ds(0, rows)
     begun = [project(i, hd, whole) for i in (1, 2)]
     for k in range(nhead - 1):
         x_copy(k).wait_recv()
-        w_copy(k).start()
     for k in range(1, nhead):
         other = (hd + k) % nhead
         begun = [b + project(i, other, whole) for b, i in zip(begun, (1, 2))]
@@ -168,14 +182,14 @@
         tile = tiled(query, h)
         qs[h] = jnp.where(mine(h), tile, jnp.zeros_like(tile))
 
+    get_rows.wait()
     line = lax.broadcasted_iota(jnp.int32, (rows, blk), 0)
     for j in range(reach):
         pick = jnp.where(line == rows_ref[j:j + 1, :], 1.0, 0.0).astype(BF16)
-        for k in range(nhead):
-            got = lax.dot_general(
-                pick, table[k, pl.ds(0, rows), :], (((0,), (0,)), ((), ())), preferred_element_type=F32
-            )
-            chosen[j, k] = got.astype(BF16)
+        got = lax.dot_general(
+            pick, table[hd, pl.ds(0, rows), :], (((0,), (0,)), ((), ())), preferred_element_type=F32
+        )
+        chosen[j] = got.astype(BF16)
         b_copy(j).start()
 
     factor = scale * math.log2(math.e)
@@ -195,6 +209,12 @@
             )
             mx[h] = new
 
+    get_out.wait()
+    for k in range(nhead):
+        wsend[k] = wout_ref[:, k * cols:(k + 1) * cols]
+    wo[hd] = wsend[hd]
+    for k in range(nhead - 1):
+        w_copy(k).start()
     for ch in range(2):
         sib_copy(0, 0, ch).wait_recv()
     attend(0)
@@ -231,6 +251,15 @@
     arrive(s, True)
     for j in range(reach):
         b_copy(j).wait_recv()
+        for k in range(nhead - 1):
+            c_copy(j, k).start()
+    attend(2 * s)
+    get_live.wait()
+    get_msg.wait()
+    get_tiles.wait()
+    for j in range(reach):
+        for k in range(nhead - 1):
+            c_copy(j, k).wait_recv()
     for r in range(row_blocks):
         total = [jnp.zeros((blk, cols), F32) for _ in range(nhead)]
         for t in range(slots):
@@ -246,8 +275,7 @@
             sent = sent + jnp.dot(
                 total[k].astype(BF16), wmsg_ref[k * cols:(k + 1) * cols, :], preferred_element_type=F32
             )
-        msg[r * blk:(r + 1) * blk, :] = jnp.maximum(sent, 0.0) + x_ref[r * blk:(r + 1) * blk, :].astype(F32)
-    attend(2 * s)
+        msg[r * blk:(r + 1) * blk, :] = jnp.maximum(sent, 0.0) + table[hd, r * blk:(r + 1) * blk, :].astype(F32)
     for ch in range(2):
         ring_copy(steps, ch, ch).wait_recv()
         sib_copy(steps, 0, ch).start()
@@ -280,6 +308,8 @@
         h_copy(k).wait_send()
     for j in range(reach):
         b_copy(j).wait_send()
+        for k in range(nhead - 1):
+            c_copy(j, k).wait_send()
     for ch in range(2):
         sib_copy(0, 0, ch).wait_send()
         sib_copy(steps, 0, ch).wait_send()
@@ -322,11 +352,18 @@
     return pl.pallas_call(
         functools.partial(body, ndom, nhead, 1.0 / math.sqrt(DEPTH)),
         out_shape=jax.ShapeDtypeStruct((rows, cols), BF16),
-        in_specs=[vmem] * 7,
+        in_specs=[pl.BlockSpec(memory_space=pltpu.HBM)] * 7,
         out_specs=vmem,
         scratch_shapes=[
+            pltpu.VMEM(live.shape, jnp.int32),
+            pltpu.VMEM(tile_vals.shape, BF16),
+            pltpu.VMEM(send_rows.shape[1:], jnp.int32),
+            pltpu.VMEM(w_msg.shape, BF16),
+            pltpu.VMEM(w_qkv.shape, BF16),
+            pltpu.VMEM(w_out.shape, BF16),
+            dma((7,)),
             pltpu.VMEM((nhead, rows + reach * blk, cols), BF16),
-            pltpu.VMEM((reach, nhead, blk, cols), BF16),
+            pltpu.VMEM((reach, blk, cols), BF16),
             pltpu.VMEM((nhead, width, cols), BF16),
             pltpu.VMEM((nhead, width, cols), BF16),
             pltpu.VMEM((2 * steps, 2, rows, 2 * width), BF16),
@@ -338,12 +375,13 @@
             dma((others,)), dma((others,)),
             dma((others,)), dma((others,)),
             dma((reach,)), dma((reach,)),
+            dma((reach, others)), dma((reach, others)),
             dma((steps + 1, 2, 2)), dma((steps + 1, 2, 2)),
             dma((steps + 1, 2, 2)), dma((steps + 1, 2, 2)),
             dma((others,)), dma((others,)),
         ],
         compiler_params=pltpu.CompilerParams(
-            collective_id=0, has_side_effects=True, vmem_limit_bytes=48 * 1024 * 1024
+            collective_id=0, has_side_effects=True, vmem_limit_bytes=63 * 1024 * 1024
         ),
     )(live, node_feats, tile_vals, send_rows[0], w_msg, w_qkv, w_out)
 

time: 70.9 us -> 67 us (0.945)
  local copies, waits for them, and re-layouts: 7.05 us -> 3.03 us
    unnamed x15 -> x3, local copies, waits for them, and re-layouts: 6.9 us -> 2.27 us
where the time goes in v2:
time: 67 us; the launch traced here: 66.9 us
  Pallas kernels  63.1 us (94%)
  local copies, waits for them, and re-layouts  3.03 us (5%)
  other arithmetic  0.75 us (1%)
    pallas_call x1, Pallas kernels, local(): pl.pallas_call(functools.partial(body, ndom, nhead, 1.0 / math.sqrt(DEPTH...  63.1 us
    unnamed x3, local copies, waits for them, and re-layouts  2.27 us

profile of v2, /device:TPU:0, one launch (start us, length us, event | category | flops | bytes accessed | tf_op | source)
XLA Modules:
  0.0 66.9 jit_solution(16014451520424817543)
XLA Ops:
  0.0 0.0 copy-start
  0.0 0.7 copy-done
  0.7 0.8 %fusion = s32[3,4]{1,0:T(4,128)S(1)} fusion(s32[3,4]{1,0:T(4,128)} %param.11, s32[3]{0:T(128)S(1)} %copy-done), kind=kLoop, calls=%fused_computation.1 | loop fusion | flops 24 | bytes 108 | tf_op jit(solution)/shard_map/jit(_where)/select_n | solution.py:350
  1.4 0.1 broadcast_in_dim.13
  1.5 0.7 %broadcast_in_dim.14.live_in = s32[12,128]{1,0:T(8,128)} broadcast(s32[12]{0:T(128)S(1)} %broadcast_in_dim.13), dimensions={0} | broadcast | bytes 6192 | tf_op jit(solution)/shard_map/broadcast_in_dim | solution.py:351
  2.2 63.1 %shard_map.82 = bf16[384,256]{1,0:T(8,128)(2,1)} custom-call(s32[12,128]{1,0:T(8,128)} %broadcast_in_dim.14.live_in, bf16[384,256]{1,0:T(8,128)(2,1)} %x_ref.1, bf16[3,4,128,128]{3,2,1,0:T(8,128)(2,1)} %tiles_in.1, s32[4,128]{1,0:T(4,128)} %bitcast.1, bf16[512,256]{1,0:T(8,128)(2,1)} %wmsg_in.1, bf16[3,512,256]{2,1,0:T(8,128)(2,1)} %wqkv_in.1, ...), custom_call_target="tpu_custom_call" | custom-call | tf_op jit(solution)/shard_map/pallas_call | solution.py:352
  65.2 1.6 %copy.10 = bf16[384,256]{1,0:T(8,128)(2,1)} copy(bf16[384,256]{1,0:T(8,128)(2,1)} %shard_map.82) | data formatting | bytes 393216
Async XLA Ops:
  0.0 0.7 copy-start

commit v3 on v2

--- a/solution.py
+++ b/solution.py
@@ -51,6 +51,7 @@
     table, chosen, wsend, wo, kv, qs, mx, acc, hg, msg,
     x_send, x_recv, w_send, w_recv, b_send, b_recv, c_send, c_recv,
     r_send, r_recv, s_send, s_recv, h_send, h_recv,
+    f_send, f_recv, fx,
 ):
     rows, cols = x_ref.shape
     width = qs.shape[2] * (kv.shape[3] // (2 * LANES))
@@ -118,6 +119,9 @@
 
     def ring_copy(s, way, ch):
         to = right if way == 0 else left
+        if ch == 1:
+            src = x_ref.at[part(1)] if isinstance(s, int) and s == 1 else fx.at[s - 1, way, hd]
+            return copy(src, fx.at[s, way, hd], r_send.at[s, way, ch], r_recv.at[s, way, ch], to)
         if isinstance(s, int) and s == 1:
             src = kv.at[0, 0, part(ch)]
         else:
@@ -128,6 +132,10 @@
             dst = kv.at[2 * s, way, part(ch)]
         return copy(src, dst, r_send.at[s, way, ch], r_recv.at[s, way, ch], to)
 
+    def f_copy(s, way, k):
+        both = fx.at[s, way, hd]
+        return copy(both, both, f_send.at[s, way, k], f_recv.at[s, way, k], peers[k])
+
     def sib_copy(s, way, ch):
         if isinstance(s, int) and s == 0:
             src, dst = kv.at[0, 0, part(ch)], kv.at[0, 1, part(ch)]
@@ -139,6 +147,8 @@
 
     for k in range(nhead - 1):
         x_copy(k).start()
+    for way in range(2):
+        ring_copy(1, way, 1).start()
 
     def project(which, k, rs):
         w = wqkv_ref[which, pl.ds(pl.multiple_of(k * cols, cols), cols), :]
@@ -166,7 +176,8 @@
         for i in range(2):
             kv[0, 0, part(ch), i * width:(i + 1) * width] = begun[i][ch * half:(ch + 1) * half].astype(BF16)
         for way in range(2):
-            ring_copy(1, way, ch).start()
+            if ch == 0:
+                ring_copy(1, way, ch).start()
         sib_copy(0, 0, ch).start()
 
     lane = lax.broadcasted_iota(jnp.int32, (1, LANES), 1)
@@ -220,12 +231,35 @@
     attend(0)
 
     def arrive(s, last):
-        for ch in range(2):
+        for ch in (1, 0):
             for way in range(2):
                 ring_copy(s, way, ch).wait_recv()
                 if not last or way == ch:
                     ring_copy_next(s, way, ch, last).start()
-                sib_copy(s, way, ch).start()
+                if ch == 0:
+                    sib_copy(s, way, ch).start()
+                else:
+                    for k in range(nhead - 1):
+                        f_copy(s, way, k).start()
+
+    def projected(s, way):
+        for k in range(nhead - 1):
+            f_copy(s, way, k).wait_recv()
+        made = []
+        for i in (1, 2):
+            total = jnp.zeros((half, width), F32)
+            for k in range(nhead):
+                w = wqkv_ref[i, k * cols:(k + 1) * cols, :]
+                total = total + jnp.dot(fx[s, way, k], w, preferred_element_type=F32)
+            made.append(total.astype(BF16))
+        return made
+
+    def digest(s):
+        for way in range(2):
+            made = projected(s, way)
+            for i in range(2):
+                kv[2 * s, way, part(1), i * width:(i + 1) * width] = made[i]
+            sib_copy(s, way, 1).start()
 
     def ring_copy_next(s, way, ch, last):
         if last:
@@ -238,14 +272,19 @@
                 sib_copy(s, way, ch).wait_recv()
 
     def turn(i, carry):
-        s = i + 1
+        s = i + 2
         arrive(s, False)
+        attend(2 * s - 1)
+        digest(s)
         attend(2 * s)
         taken(s)
-        attend(2 * s + 1)
         return carry
 
-    lax.fori_loop(0, steps - 2, turn, 0)
+    arrive(1, False)
+    digest(1)
+    attend(2)
+    taken(1)
+    lax.fori_loop(0, steps - 3, turn, 0)
 
     s = steps - 1
     arrive(s, True)
@@ -253,6 +292,8 @@
         b_copy(j).wait_recv()
         for k in range(nhead - 1):
             c_copy(j, k).start()
+    attend(2 * s - 1)
+    digest(s)
     attend(2 * s)
     get_live.wait()
     get_msg.wait()
@@ -276,11 +317,17 @@
                 total[k].astype(BF16), wmsg_ref[k * cols:(k + 1) * cols, :], preferred_element_type=F32
             )
         msg[r * blk:(r + 1) * blk, :] = jnp.maximum(sent, 0.0) + table[hd, r * blk:(r + 1) * blk, :].astype(F32)
-    for ch in range(2):
-        ring_copy(steps, ch, ch).wait_recv()
-        sib_copy(steps, 0, ch).start()
+    ring_copy(steps, 1, 1).wait_recv()
+    for k in range(nhead - 1):
+        f_copy(steps, 1, k).start()
+    ring_copy(steps, 0, 0).wait_recv()
+    sib_copy(steps, 0, 0).start()
     taken(s)
     attend(2 * s + 1)
+    made = projected(steps, 1)
+    for i in range(2):
+        kv[1, 0, part(1), i * width:(i + 1) * width] = made[i]
+    sib_copy(steps, 0, 1).start()
     for ch in range(2):
         sib_copy(steps, 0, ch).wait_recv()
     attend(1)
@@ -306,6 +353,7 @@
         x_copy(k).wait_send()
         w_copy(k).wait_send()
         h_copy(k).wait_send()
+        f_copy(steps, 1, k).wait_send()
     for j in range(reach):
         b_copy(j).wait_send()
         for k in range(nhead - 1):
@@ -321,6 +369,9 @@
         for ch in range(2):
             for way in range(2):
                 sib_copy(i + 1, way, ch).wait_send()
+        for k in range(nhead - 1):
+            for way in range(2):
+                f_copy(i + 1, way, k).wait_send()
         return carry
 
     def sent_ring(i, carry):
@@ -379,6 +430,8 @@
             dma((steps + 1, 2, 2)), dma((steps + 1, 2, 2)),
             dma((steps + 1, 2, 2)), dma((steps + 1, 2, 2)),
             dma((others,)), dma((others,)),
+            dma((steps + 1, 2, others)), dma((steps + 1, 2, others)),
+            pltpu.VMEM((steps + 1, 2, nhead, rows // 2, cols), BF16),
         ],
         compiler_params=pltpu.CompilerParams(
             collective_id=0, has_side_effects=True, vmem_limit_bytes=63 * 1024 * 1024

time: 67 us -> 68 us (1.015)
  Pallas kernels: 63.1 us -> 63.9 us
    pallas_call x1, Pallas kernels: 63.1 us -> 63.9 us  [local(): pl.pallas_call(functools.partial(body, ndom, nhead, 1.0 / math.sqrt(DEPTH...]
where the time goes in v3:
time: 68 us; the launch traced here: 67.7 us
  Pallas kernels  63.9 us (94%)
  local copies, waits for them, and re-layouts  3.03 us (4%)
  other arithmetic  0.75 us (1%)
    pallas_call x1, Pallas kernels, local(): pl.pallas_call(functools.partial(body, ndom, nhead, 1.0 / math.sqrt(DEPTH...  63.9 us
    unnamed x3, local copies, waits for them, and re-layouts  2.27 us

profile of v3, /device:TPU:0, one launch (start us, length us, event | category | flops | bytes accessed | tf_op | source)
XLA Modules:
  0.0 67.7 jit_solution(18331856742154632307)
XLA Ops:
  0.0 0.0 copy-start
  0.0 0.7 copy-done
  0.7 0.8 %fusion = s32[3,4]{1,0:T(4,128)S(1)} fusion(s32[3,4]{1,0:T(4,128)} %param.11, s32[3]{0:T(128)S(1)} %copy-done), kind=kLoop, calls=%fused_computation.1 | loop fusion | flops 24 | bytes 108 | tf_op jit(solution)/shard_map/jit(_where)/select_n | solution.py:401
  1.4 0.1 broadcast_in_dim.13
  1.5 0.7 broadcast_in_dim.14.live_in
  2.2 63.9 %shard_map.82 = bf16[384,256]{1,0:T(8,128)(2,1)} custom-call(s32[12,128]{1,0:T(8,128)} %broadcast_in_dim.14.live_in, bf16[384,256]{1,0:T(8,128)(2,1)} %x_ref.1, bf16[3,4,128,128]{3,2,1,0:T(8,128)(2,1)} %tiles_in.1, s32[4,128]{1,0:T(4,128)} %bitcast.1, bf16[512,256]{1,0:T(8,128)(2,1)} %wmsg_in.1, bf16[3,512,256]{2,1,0:T(8,128)(2,1)} %wqkv_in.1, ...), custom_call_target="tpu_custom_call" | custom-call | tf_op jit(solution)/shard_map/pallas_call | solution.py:403
  66.1 1.6 %copy.10 = bf16[384,256]{1,0:T(8,128)(2,1)} copy(bf16[384,256]{1,0:T(8,128)(2,1)} %shard_map.82) | data formatting | bytes 393216
Async XLA Ops:
  0.0 0.7 copy-start

commit v4 on v2

--- a/solution.py
+++ b/solution.py
@@ -254,6 +254,11 @@
         for k in range(nhead - 1):
             c_copy(j, k).start()
     attend(2 * s)
+    for ch in range(2):
+        ring_copy(steps, ch, ch).wait_recv()
+        sib_copy(steps, 0, ch).start()
+    taken(s)
+    attend(2 * s + 1)
     get_live.wait()
     get_msg.wait()
     get_tiles.wait()
@@ -276,11 +281,6 @@
                 total[k].astype(BF16), wmsg_ref[k * cols:(k + 1) * cols, :], preferred_element_type=F32
             )
         msg[r * blk:(r + 1) * blk, :] = jnp.maximum(sent, 0.0) + table[hd, r * blk:(r + 1) * blk, :].astype(F32)
-    for ch in range(2):
-        ring_copy(steps, ch, ch).wait_recv()
-        sib_copy(steps, 0, ch).start()
-    taken(s)
-    attend(2 * s + 1)
     for ch in range(2):
         sib_copy(steps, 0, ch).wait_recv()
     attend(1)

time: 67 us -> 65 us (0.970)
  Pallas kernels: 63.1 us -> 61.1 us
    pallas_call x1, Pallas kernels: 63.1 us -> 61.1 us  [local(): pl.pallas_call(functools.partial(body, ndom, nhead, 1.0 / math.sqrt(DEPTH...]
where the time goes in v4:
time: 65 us; the launch traced here: 64.9 us
  Pallas kernels  61.1 us (94%)
  local copies, waits for them, and re-layouts  3.03 us (5%)
  other arithmetic  0.75 us (1%)
    pallas_call x1, Pallas kernels, local(): pl.pallas_call(functools.partial(body, ndom, nhead, 1.0 / math.sqrt(DEPTH...  61.1 us
    unnamed x3, local copies, waits for them, and re-layouts  2.27 us

profile of v4, /device:TPU:0, one launch (start us, length us, event | category | flops | bytes accessed | tf_op | source)
XLA Modules:
  0.0 64.9 jit_solution(16506892191132292809)
XLA Ops:
  0.0 0.0 copy-start
  0.0 0.7 %copy-done = s32[3]{0:T(128)S(1)} copy-done((s32[3]{0:T(128)S(1)}, s32[3]{0:T(128)}, u32[]{:S(2)}) %copy-start) | copy-done | bytes 36
  0.7 0.8 %fusion = s32[3,4]{1,0:T(4,128)S(1)} fusion(s32[3,4]{1,0:T(4,128)} %param.11, s32[3]{0:T(128)S(1)} %copy-done), kind=kLoop, calls=%fused_computation.1 | loop fusion | flops 24 | bytes 108 | tf_op jit(solution)/shard_map/jit(_where)/select_n | solution.py:350
  1.4 0.1 broadcast_in_dim.13
  1.5 0.7 %broadcast_in_dim.14.live_in = s32[12,128]{1,0:T(8,128)} broadcast(s32[12]{0:T(128)S(1)} %broadcast_in_dim.13), dimensions={0} | broadcast | bytes 6192 | tf_op jit(solution)/shard_map/broadcast_in_dim | solution.py:351
  2.2 61.1 %shard_map.82 = bf16[384,256]{1,0:T(8,128)(2,1)} custom-call(s32[12,128]{1,0:T(8,128)} %broadcast_in_dim.14.live_in, bf16[384,256]{1,0:T(8,128)(2,1)} %x_ref.1, bf16[3,4,128,128]{3,2,1,0:T(8,128)(2,1)} %tiles_in.1, s32[4,128]{1,0:T(4,128)} %bitcast.1, bf16[512,256]{1,0:T(8,128)(2,1)} %wmsg_in.1, bf16[3,512,256]{2,1,0:T(8,128)(2,1)} %wqkv_in.1, ...), custom_call_target="tpu_custom_call" | custom-call | tf_op jit(solution)/shard_map/pallas_call | solution.py:352
  63.3 1.6 %copy.10 = bf16[384,256]{1,0:T(8,128)(2,1)} copy(bf16[384,256]{1,0:T(8,128)(2,1)} %shard_map.82) | data formatting | bytes 393216
Async XLA Ops:
  0.0 0.7 %copy-start = (s32[3]{0:T(128)S(1)}, s32[3]{0:T(128)}, u32[]{:S(2)}) copy-start(s32[3]{0:T(128)} %param.10) | copy-start | bytes 40
